TPU v7x, 32 devices: a whole 2x2x4 slice. The times are simulated.
32 devices in a mesh: dp: 4 (over y, core), fsdp: 8 (over z, x).
Axes of the slice: x: 2, y: 2, z: 4, core: 2. Of those that a mesh axis runs over, the one named last changes fastest.
Arguments:
- frames: bfloat16 [16384, 768], P(('dp', 'fsdp')), may hold values from -6 to 6
- lengths: int32 [32, 2], P(('dp', 'fsdp')), may hold values from 0 to 512, as said below
- query_weight: bfloat16 [768, 768], P(('dp', 'fsdp')), may hold values from -0.21875 to 0.21875
- query_bias: bfloat16 [768], P(('dp', 'fsdp')), may hold values from -3 to 3
- key_weight: bfloat16 [768, 768], P(('dp', 'fsdp')), may hold values from -0.21875 to 0.21875
- value_weight: bfloat16 [768, 768], P(('dp', 'fsdp')), may hold values from -0.21875 to 0.21875
- value_bias: bfloat16 [768], P(('dp', 'fsdp')), may hold values from -3 to 3
- output_weight: bfloat16 [768, 768], P(('dp', 'fsdp')), may hold values from -2.5 to 2.5
- output_bias: bfloat16 [768], P(('dp', 'fsdp')), may hold values from -3 to 3
- first_gain: bfloat16 [768], P(('dp', 'fsdp')), may hold values from 0.5 to 1.5
- first_shift: bfloat16 [768], P(('dp', 'fsdp')), may hold values from -3 to 3
- inner_weight: bfloat16 [768, 3072], P(('dp', 'fsdp')), may hold values from -0.21875 to 0.21875
- inner_bias: bfloat16 [3072], P(('dp', 'fsdp')), may hold values from -3 to 3
- outer_weight: bfloat16 [3072, 768], P(('dp', 'fsdp')), may hold values from -0.109375 to 0.109375
- outer_bias: bfloat16 [768], P(('dp', 'fsdp')), may hold values from -3 to 3
- second_gain: bfloat16 [768], P(('dp', 'fsdp')), may hold values from 0.5 to 1.5
- second_shift: bfloat16 [768], P(('dp', 'fsdp')), may hold values from -3 to 3
- grad_out: bfloat16 [16384, 768], P(('dp', 'fsdp')), may hold values from -6 to 6
Outputs:
- layer_out: bfloat16 [16384, 768], P(('dp', 'fsdp'))
- frames_grad: bfloat16 [16384, 768], P(('dp', 'fsdp'))
- query_weight_grad: float32 [768, 768], P(('dp', 'fsdp'))
- query_bias_grad: float32 [768], P(('dp', 'fsdp'))
- key_weight_grad: float32 [768, 768], P(('dp', 'fsdp'))
- value_weight_grad: float32 [768, 768], P(('dp', 'fsdp'))
- value_bias_grad: float32 [768], P(('dp', 'fsdp'))
- output_weight_grad: float32 [768, 768], P(('dp', 'fsdp'))
- output_bias_grad: float32 [768], P(('dp', 'fsdp'))
- first_gain_grad: float32 [768], P(('dp', 'fsdp'))
- first_shift_grad: float32 [768], P(('dp', 'fsdp'))
- inner_weight_grad: float32 [768, 3072], P(('dp', 'fsdp'))
- inner_bias_grad: float32 [3072], P(('dp', 'fsdp'))
- outer_weight_grad: float32 [3072, 768], P(('dp', 'fsdp'))
- outer_bias_grad: float32 [768], P(('dp', 'fsdp'))
- second_gain_grad: float32 [768], P(('dp', 'fsdp'))
- second_shift_grad: float32 [768], P(('dp', 'fsdp'))
Inputs may be any that keep to these rules, and one draw needn't show every extreme that they name: `lengths`: row b holds block b's two utterances: slot 0 has 100 to 512 frames, slot 1 has 0 (empty) up to 512 minus slot 0; the block's remaining slots are padding. In one block, drawn from the seed, slot 0 fills all 512 slots.
All inputs are finite; a program needn't handle non-finite values.
Results may differ from a plain program's by a relative error of at most 0.015.
Values may be sent and summed in bfloat16 or wider, within the bound.
A program may use at most 192 MiB of HBM per device.

v0:
```python
import functools
from types import SimpleNamespace

import jax
import jax.numpy as jnp
from jax import lax
from jax.experimental import pallas as pl
from jax.experimental.pallas import tpu as pltpu
from jax.sharding import PartitionSpec as P

HEADS = 12


def layer_norm(values, gain_vec, shift_vec):
    center = values - jnp.mean(values, axis=-1, keepdims=True)
    spread = jnp.mean(center * center, axis=-1, keepdims=True)
    return center * lax.rsqrt(spread + 1e-05) * gain_vec + shift_vec


def exact_gelu(values):
    return jax.nn.gelu(values, approximate=False)


def matmul(left_side, right_side):
    return jnp.dot(left_side, right_side, preferred_element_type=jnp.float32)


def matmul_tn(left_side, right_side):
    return lax.dot_general(
        left_side, right_side, (((0,), (0,)), ((), ())), preferred_element_type=jnp.float32
    )


def matmul_nt(left_side, right_side):
    return lax.dot_general(
        left_side, right_side, (((1,), (1,)), ((), ())), preferred_element_type=jnp.float32
    )


def column_sums(values):
    return jnp.sum(values.astype(jnp.float32), axis=0)


def block_scores(query_block, key_heads, group_block, groups, score_scale):
    raw_scores = (
        jnp.einsum("qhd,khd->hqk", query_block, key_heads, preferred_element_type=jnp.float32)
        * score_scale
    )
    allowed = group_block[:, None] == groups[None, :]
    return jnp.where(allowed[None], raw_scores, -1e30)


def general_device(
    frames,
    lengths,
    query_weight,
    query_bias,
    key_weight,
    value_weight,
    value_bias,
    output_weight,
    output_bias,
    first_gain,
    first_shift,
    inner_weight,
    inner_bias,
    outer_weight,
    outer_bias,
    second_gain,
    second_shift,
    grad_out,
):
    frame_count = frames.shape[0]
    model_width = frames.shape[1]
    head_size = model_width // HEADS
    score_scale = head_size ** (-0.5)
    places = jnp.arange(frame_count, dtype=jnp.int32)
    bounds = jnp.stack([lengths[0, 0], lengths[0, 0] + lengths[0, 1]])
    groups = jnp.sum((places[:, None] >= bounds[None, :]).astype(jnp.int32), axis=1)
    live_mask = (places < bounds[-1]).astype(jnp.float32)
    gathered = (
        lax.all_gather(query_weight, ("dp", "fsdp"), axis=0, tiled=True),
        lax.all_gather(query_bias, ("dp", "fsdp"), axis=0, tiled=True),
        lax.all_gather(key_weight, ("dp", "fsdp"), axis=0, tiled=True),
        lax.all_gather(value_weight, ("dp", "fsdp"), axis=0, tiled=True),
        lax.all_gather(value_bias, ("dp", "fsdp"), axis=0, tiled=True),
        lax.all_gather(output_weight, ("dp", "fsdp"), axis=0, tiled=True),
        lax.all_gather(output_bias, ("dp", "fsdp"), axis=0, tiled=True),
        lax.all_gather(first_gain, ("dp", "fsdp"), axis=0, tiled=True),
        lax.all_gather(first_shift, ("dp", "fsdp"), axis=0, tiled=True),
        lax.all_gather(inner_weight, ("dp", "fsdp"), axis=0, tiled=True),
        lax.all_gather(inner_bias, ("dp", "fsdp"), axis=0, tiled=True),
        lax.all_gather(outer_weight, ("dp", "fsdp"), axis=0, tiled=True),
        lax.all_gather(outer_bias, ("dp", "fsdp"), axis=0, tiled=True),
        lax.all_gather(second_gain, ("dp", "fsdp"), axis=0, tiled=True),
        lax.all_gather(second_shift, ("dp", "fsdp"), axis=0, tiled=True),
    )
    (
        query_mat,
        query_vec,
        key_mat,
        value_mat,
        value_vec,
        output_mat,
        output_vec,
        first_scale,
        first_offset,
        inner_mat,
        inner_vec,
        outer_mat,
        outer_vec,
        second_scale,
        second_offset,
    ) = gathered
    query_rows = (matmul(frames, query_mat) + query_vec.astype(jnp.float32)).astype(jnp.bfloat16)
    key_rows = matmul(frames, key_mat).astype(jnp.bfloat16)
    value_rows = (matmul(frames, value_mat) + value_vec.astype(jnp.float32)).astype(jnp.bfloat16)
    query_heads = query_rows.reshape(frame_count, HEADS, head_size)
    key_heads = key_rows.reshape(frame_count, HEADS, head_size)
    value_heads = value_rows.reshape(frame_count, HEADS, head_size)
    scores = block_scores(query_heads, key_heads, groups, groups, score_scale)
    row_max = jnp.max(scores, axis=-1, keepdims=True)
    raw_weights = jnp.exp(scores - row_max)
    row_total = jnp.sum(raw_weights, axis=-1, keepdims=True)
    attn_prob = raw_weights / row_total
    log_totals = row_max + jnp.log(row_total)
    context_parts = jnp.einsum(
        "hqk,khd->qhd",
        attn_prob.astype(jnp.bfloat16),
        value_heads,
        preferred_element_type=jnp.float32,
    )
    context_rows = context_parts.reshape(frame_count, model_width).astype(jnp.bfloat16)
    frames_float = frames.astype(jnp.float32)
    resid_one = frames_float + matmul(context_rows, output_mat) + output_vec.astype(jnp.float32)
    hidden, first_pull = jax.vjp(
        layer_norm, resid_one, first_scale.astype(jnp.float32), first_offset.astype(jnp.float32)
    )
    hidden_low = hidden.astype(jnp.bfloat16)
    inner_pre = matmul(hidden_low, inner_mat) + inner_vec.astype(jnp.float32)
    active, gelu_pull = jax.vjp(exact_gelu, inner_pre)
    active_low = active.astype(jnp.bfloat16)
    outer_out = matmul(active_low, outer_mat) + outer_vec.astype(jnp.float32)
    normed_out, second_pull = jax.vjp(
        layer_norm,
        hidden + outer_out,
        second_scale.astype(jnp.float32),
        second_offset.astype(jnp.float32),
    )
    layer_out = (normed_out * live_mask[:, None]).astype(jnp.bfloat16)
    grad_top = grad_out.astype(jnp.float32) * live_mask[:, None]
    grad_two, second_gain_grad, second_shift_grad = second_pull(grad_top)
    grad_outer = grad_two.astype(jnp.bfloat16)
    outer_mat_grad = matmul_tn(active_low, grad_outer)
    outer_vec_grad = column_sums(grad_outer)
    (grad_inner,) = gelu_pull(matmul_nt(grad_outer, outer_mat))
    grad_inner_low = grad_inner.astype(jnp.bfloat16)
    inner_mat_grad = matmul_tn(hidden_low, grad_inner_low)
    inner_vec_grad = column_sums(grad_inner_low)
    grad_hidden = grad_two + matmul_nt(grad_inner_low, inner_mat)
    grad_one, first_gain_grad, first_shift_grad = first_pull(grad_hidden)
    grad_attn = grad_one.astype(jnp.bfloat16)
    output_mat_grad = matmul_tn(context_rows, grad_attn)
    output_vec_grad = column_sums(grad_attn)
    grad_context = (
        matmul_nt(grad_attn, output_mat).astype(jnp.bfloat16).reshape(frame_count, HEADS, head_size)
    )
    scores = block_scores(query_heads, key_heads, groups, groups, score_scale)
    attn_prob = jnp.exp(scores - log_totals)
    grad_prob = jnp.einsum(
        "qhd,khd->hqk", grad_context, value_heads, preferred_element_type=jnp.float32
    )
    inner_sum = jnp.sum(attn_prob * grad_prob, axis=-1, keepdims=True)
    grad_scores = (attn_prob * (grad_prob - inner_sum)).astype(jnp.bfloat16)
    query_grad_parts = (
        jnp.einsum("hqk,khd->qhd", grad_scores, key_heads, preferred_element_type=jnp.float32)
        * score_scale
    )
    key_grad_sum = (
        jnp.einsum("hqk,qhd->khd", grad_scores, query_heads, preferred_element_type=jnp.float32)
        * score_scale
    )
    value_grad_sum = jnp.einsum(
        "hqk,qhd->khd",
        attn_prob.astype(jnp.bfloat16),
        grad_context,
        preferred_element_type=jnp.float32,
    )
    grad_query = query_grad_parts.reshape(frame_count, model_width).astype(jnp.bfloat16)
    grad_key = key_grad_sum.reshape(frame_count, model_width).astype(jnp.bfloat16)
    grad_value = value_grad_sum.reshape(frame_count, model_width).astype(jnp.bfloat16)
    query_mat_grad = matmul_tn(frames, grad_query)
    query_vec_grad = column_sums(grad_query)
    key_mat_grad = matmul_tn(frames, grad_key)
    value_mat_grad = matmul_tn(frames, grad_value)
    value_vec_grad = column_sums(grad_value)
    frames_grad = (
        grad_one
        + matmul_nt(grad_query, query_mat)
        + matmul_nt(grad_key, key_mat)
        + matmul_nt(grad_value, value_mat)
    ).astype(jnp.bfloat16)
    shares = (
        lax.psum_scatter(query_mat_grad, ("dp", "fsdp"), scatter_dimension=0, tiled=True),
        lax.psum_scatter(query_vec_grad, ("dp", "fsdp"), scatter_dimension=0, tiled=True),
        lax.psum_scatter(key_mat_grad, ("dp", "fsdp"), scatter_dimension=0, tiled=True),
        lax.psum_scatter(value_mat_grad, ("dp", "fsdp"), scatter_dimension=0, tiled=True),
        lax.psum_scatter(value_vec_grad, ("dp", "fsdp"), scatter_dimension=0, tiled=True),
        lax.psum_scatter(output_mat_grad, ("dp", "fsdp"), scatter_dimension=0, tiled=True),
        lax.psum_scatter(output_vec_grad, ("dp", "fsdp"), scatter_dimension=0, tiled=True),
        lax.psum_scatter(first_gain_grad, ("dp", "fsdp"), scatter_dimension=0, tiled=True),
        lax.psum_scatter(first_shift_grad, ("dp", "fsdp"), scatter_dimension=0, tiled=True),
        lax.psum_scatter(inner_mat_grad, ("dp", "fsdp"), scatter_dimension=0, tiled=True),
        lax.psum_scatter(inner_vec_grad, ("dp", "fsdp"), scatter_dimension=0, tiled=True),
        lax.psum_scatter(outer_mat_grad, ("dp", "fsdp"), scatter_dimension=0, tiled=True),
        lax.psum_scatter(outer_vec_grad, ("dp", "fsdp"), scatter_dimension=0, tiled=True),
        lax.psum_scatter(second_gain_grad, ("dp", "fsdp"), scatter_dimension=0, tiled=True),
        lax.psum_scatter(second_shift_grad, ("dp", "fsdp"), scatter_dimension=0, tiled=True),
    )
    return (
        layer_out,
        frames_grad,
        shares[0],
        shares[1],
        shares[2],
        shares[3],
        shares[4],
        shares[5],
        shares[6],
        shares[7],
        shares[8],
        shares[9],
        shares[10],
        shares[11],
        shares[12],
        shares[13],
        shares[14],
    )


MESH = pl.DeviceIdType.MESH
NZ = 4
LANES = 128


class Net:
    def __init__(self):
        dp, fs = lax.axis_index("dp"), lax.axis_index("fsdp")
        self.y, self.c = lax.div(dp, 2), lax.rem(dp, 2)
        self.z, self.x = lax.div(fs, 2), lax.rem(fs, 2)

    def dev(self, y=None, c=None, z=None, x=None):
        y = self.y if y is None else y
        c = self.c if c is None else c
        z = self.z if z is None else z
        x = self.x if x is None else x
        return (y * 2 + c, z * 2 + x)

    def across(self, dim):
        if dim == "x":
            return self.dev(x=1 - self.x)
        if dim == "y":
            return self.dev(y=1 - self.y)
        return self.dev(c=1 - self.c)

    def greet(self):
        bar = pltpu.get_barrier_semaphore()

        def tell(device):
            pl.semaphore_signal(bar, inc=1, device_id=device, device_id_type=MESH)

        for dim in "xyc":
            tell(self.across(dim))
        for k in range(1, NZ):
            tell(self.dev(z=lax.rem(self.z + k, NZ)))

    def meet(self):
        pl.semaphore_wait(pltpu.get_barrier_semaphore(), 3 + NZ - 1)


class Way:
    def __init__(self, net, region, order, sems):
        self.net, self.region, self.order = net, region, order
        self.out, self.mate, self.recv = sems

    def copy(self, src, dst, slot, device, send=None):
        return pltpu.make_async_remote_copy(
            src_ref=src, dst_ref=dst, send_sem=self.out if send is None else send, recv_sem=self.recv.at[slot],
            device_id=device, device_id_type=MESH)

    def wait_for(self, ref, slot):
        self.copy(ref, ref, slot, self.net.across("c")).wait_recv()

    def part(self, have="", **at):
        n = self.net
        for d in "yzx":
            at.setdefault(d, None if d in have else getattr(n, d))
        return self.region(at["y"], n.c, at["z"], at["x"])

    def flip(self, *dims):
        return {d: 1 - getattr(self.net, d) for d in dims}

    def ahead(self, k):
        return lax.rem(self.net.z + k, NZ)


class Gather(Way):
    def __init__(self, net, region, order, sems, bulk):
        super().__init__(net, region, order, sems)
        self.bulk = bulk

    def lines_start(self, have):
        part = self.part(have)
        for k in range(1, NZ):
            self.copy(part, part, 0, self.net.dev(z=self.ahead(k))).start()

    def lines_wait(self, have):
        self.wait_for(self.bulk(len(have) * (NZ - 1) + NZ - 1), 0)

    def over(self, slot, d, have, **at):
        part = self.part(have, **at)
        return self.copy(part, part, slot, self.net.across(d))

    def sibling(self):
        part = self.region(None, self.net.c, None, None)
        return self.copy(part, part, 3, self.net.across("c"), self.mate)

    def stages(self):
        first, d2, d3 = self.order

        def start_a():
            self.lines_start("")

        def start_b():
            self.lines_wait("")
            self.over(1, d2, "z").start()
            self.over(2, d3, "z").start()

        def start_c():
            self.over(1, d2, "z").wait_recv()
            self.over(2, d3, "z", **self.flip(d2)).start()

        def start_d():
            self.wait_for(self.part(d2 + "z", **self.flip(d3)), 2)
            self.sibling().start()

        def start_e():
            self.sibling().wait_recv()

        if first == "z":
            return dict(a=start_a, b=start_b, c=start_c, d=start_d, e=start_e)

        def begin_a():
            self.over(1, first, "").start()

        def begin_b():
            self.over(1, first, "").wait_recv()
            self.lines_start(first)

        def begin_c():
            self.lines_wait(first)
            self.over(2, d3, first + "z").start()

        def begin_d():
            self.wait_for(self.part(first + "z", **self.flip(d3)), 2)
            self.sibling().start()

        return dict(a=begin_a, b=begin_b, c=begin_c, d=begin_d, e=start_e)


class Scatter(Way):
    def __init__(self, net, region, order, sems, first, third, line):
        super().__init__(net, region, order, sems)
        self.into_first, self.into_third, self.into_line = first, third, line
        self.inner = order[0] != "z"
        self.near = order[0] if self.inner else order[1]
        self.far = order[2]
        self.rest = self.near + "z" if self.inner else "z"

    def sibling(self, core):
        part = self.region(None, core, None, None)
        return self.copy(part, part, 4, self.net.across("c"), self.mate)

    def sibling_out(self):
        return self.sibling(1 - self.net.c)

    def sibling_in(self):
        return self.sibling(self.net.c)

    def first(self):
        if self.inner:
            return self.copy(self.part(self.rest, **self.flip(self.far)), self.into_first, 0, self.net.across(self.far))
        part = self.part("z", **self.flip(self.far, self.near))
        return self.copy(part, self.into_first.at[0], 0, self.net.across(self.far))

    def second(self):
        part = self.part("z", **self.flip(self.far))
        return self.copy(part, self.into_first.at[1], 1, self.net.across(self.far))

    def third(self):
        part = self.part("" if self.inner else "z", **self.flip(self.near))
        return self.copy(part, self.into_third, 2, self.net.across(self.near))

    def along(self, k):
        ahead = self.ahead(k)
        part = self.part(self.near if self.inner else "", z=ahead)
        return self.copy(part, self.into_line.at[k - 1], 3, self.net.dev(z=ahead))

    @staticmethod
    def add(part, *came):
        total = part[...].astype(jnp.float32)
        for one in came:
            total = total + one[...].astype(jnp.float32)
        part[...] = total.astype(part.dtype)

    def lines_start(self):
        for k in range(1, NZ):
            self.along(k).start()

    def lines_wait(self):
        self.wait_for(self.into_line, 3)
        return [self.into_line.at[k] for k in range(NZ - 1)]

    def spread(self):
        self.first().start()
        if not self.inner:
            self.second().start()

    def fold_first(self):
        self.first().wait_recv()
        if self.inner:
            self.add(self.part(self.rest), self.into_first)
            self.lines_start()
        else:
            self.add(self.part("z", **self.flip(self.near)), self.into_first.at[0])
            self.third().start()

    def fold_second(self):
        if self.inner:
            self.add(self.part(self.near), *self.lines_wait())
            self.third().start()
        else:
            self.second().wait_recv()
            self.add(self.part("z"), self.into_first.at[1])

    def fold_third(self):
        self.third().wait_recv()
        if not self.inner:
            self.add(self.part("z"), self.into_third)
            self.lines_start()

    def total(self):
        came = [self.into_third] if self.inner else self.lines_wait()
        out = self.part()[...].astype(jnp.float32)
        for one in came:
            out = out + one[...].astype(jnp.float32)
        return out


def region_square(ref):
    pair, half = ref.shape[2] // NZ, ref.shape[3] // 2

    def region(y, c, z, x):
        rows = pl.ds(0, pair * NZ) if z is None else pl.ds(pl.multiple_of(z * pair, 16), pair)
        cols = pl.ds(0, half * 2) if x is None else pl.ds(pl.multiple_of(x * half, LANES), half)
        return ref.at[pl.ds(0, 2) if y is None else y, c, rows, cols]

    return region


def region_lead(ref, start, size):
    run = ref.shape[4] // 2

    def region(y, c, z, x):
        rows = pl.ds(0, 2 * run) if x is None else pl.ds(pl.multiple_of(x * run, 16), run)
        high, low = (pl.ds(0, 2), pl.ds(0, 2)) if z is None else (lax.div(z, 2), lax.rem(z, 2))
        return ref.at[pl.ds(0, 2) if y is None else y, c, high, low, rows, pl.ds(start, size)]

    return region


def region_small(ref):
    def region(y, c, z, x):
        return ref.at[pl.ds(0, 2) if y is None else y, c, pl.ds(0, NZ) if z is None else z, pl.ds(0, 2) if x is None else x]

    return region


def bulk_square(ref):
    pair, half = ref.shape[2] // NZ, ref.shape[3] // 2
    return lambda k: ref.at[pl.ds(0, k // 3), 0, pl.ds(0, 3 * pair), pl.ds(0, half)]


def bulk_lead(ref, start, size):
    rows = 3 * ref.shape[4] // 4
    return lambda k: ref.at[0, 0, pl.ds(0, k // 3), pl.ds(0, 2), pl.ds(0, rows), pl.ds(start, size)]


def bulk_small(ref):
    return lambda k: ref.at[0, 0, pl.ds(0, k), 0]


UNITS = range(13)
GATHER = ("zxy", "zyx", "zxy", "zyx", "yzx", "zxy", "xzy", "yzx", "zxy", "zxy", "yzx", "zyx", "zxy")
SCATTER = ("zyx", "zxy", "zxy", "yzx", "yzx", "zxy", "zxy", "zxy", "zxy", "yzx", "zxy", "xzy", "zxy")
OUTER = ((0, 256), (256, 256), (512, 128), (640, 128))


LANDING = ("first", "third", "line")


def landing_shapes(i, pair, half, run):
    order = SCATTER[i]
    if i < 8:
        piece, strip, wide = (pair, half), (pair * NZ, half), (pair * NZ, 2 * half)
        double = (pair, 2 * half)
    else:
        size = OUTER[i - 8][1]
        piece, strip, wide = (run, size), (2, 2, run, size), (2, 2, 2 * run, size)
        double = (2 * run, size)
    if order[0] == "z":
        return (2,) + strip, strip, (NZ - 1,) + piece
    if order[0] == "x":
        return wide, piece, (NZ - 1,) + double
    return (2,) + strip, piece, (NZ - 1, 2) + piece


def mm(left, right):
    return jnp.dot(left, right, preferred_element_type=jnp.float32)


def mm_nt(left, right):
    return lax.dot_general(left, right, (((1,), (1,)), ((), ())), preferred_element_type=jnp.float32)


def mm_tn(left, right):
    return lax.dot_general(left, right, (((0,), (0,)), ((), ())), preferred_element_type=jnp.float32)


def eights(block):
    return jnp.sum(block.reshape(block.shape[0] // 8, 8, block.shape[1]), axis=0)


STEP = 64
F32, BF16 = jnp.float32, jnp.bfloat16


def layer_kernel(names, *refs):
    r = SimpleNamespace(**dict(zip(names, refs, strict=True)))
    net = Net()
    frame_count, width = r.frames.shape
    half = width // 2
    lead = r.wq.shape[0]
    pair = 2 * lead
    own_rows = pl.ds(pl.multiple_of(net.z * pair, 16), pair)
    own_cols = pl.ds(pl.multiple_of(net.x * half, LANES), half)
    w8, w2 = r.w8, r.w2
    g2, e12 = r.g2, r.e12

    x_in = pltpu.make_async_copy(r.frames, r.xbuf, r.isem.at[0])
    g_in = pltpu.make_async_copy(r.grad_out, r.gbuf, r.isem.at[1])
    net.greet()
    x_in.start()
    g_in.start()

    gather, scatter = [], []
    for i in UNITS:
        cols = OUTER[i - 8] if 8 <= i < 12 else None
        if i < 8:
            region, bulk = region_square(w8.at[i]), bulk_square(w8.at[i])
            to = region_square(w2.at[i // 2, i % 2]) if i < 3 else region
        elif cols:
            region, bulk, to = region_lead(w2, *cols), bulk_lead(w2, *cols), region_lead(g2, *cols)
        else:
            region, bulk = region_small(r.small), bulk_small(r.small)
        kind = 0 if i < 8 else 1 if cols else 2
        sems = r.gout.at[kind], r.gmate.at[kind], r.grecv.at[i]
        gather.append(Gather(net, region, GATHER[i], sems, bulk).stages())
        if i < 12:
            landing = (getattr(r, f"{name}{i}") for name in LANDING)
            sems = r.sout.at[kind], r.smate.at[kind], r.srecv.at[i]
            scatter.append(Scatter(net, to, SCATTER[i], sems, *landing))

    def sent(ref, sem):
        pltpu.make_async_remote_copy(
            src_ref=ref, dst_ref=ref, send_sem=sem, recv_sem=r.grecv.at[0, 0], device_id=net.across("c"),
            device_id_type=MESH).wait_send()

    def all_sent(out, mate):
        runs = frame_count - 2 * 16
        sent(e12.at[pl.ds(0, 12), pl.ds(0, runs), pl.ds(0, half)], out.at[0])
        sent(r.act.at[pl.ds(0, 3), pl.ds(0, runs), :], out.at[1])
        sent(w8.at[:, :, 0], mate.at[0])
        sent(w2.at[:, 0], mate.at[1])

    def shard(u):
        if u < 4:
            return (r.wq, r.wk, r.wv, r.wo)[u][...]
        return r.wi[:, (u - 4) * width:(u - 3) * width]

    def swap(u):
        return pltpu.make_async_remote_copy(
            src_ref=r.xs.at[u], dst_ref=r.xr.at[u], send_sem=r.xss.at[0], recv_sem=r.xrs.at[u],
            device_id=net.across("x"), device_id_type=MESH)

    def offer(u):
        v = shard(u).astype(F32)
        theirs = jnp.where(net.x == 0, v[:, half:], v[:, :half])
        r.xs[u] = jnp.concatenate([theirs, jnp.zeros((8, half), F32)], axis=0).astype(BF16)

    def merge(u):
        swap(u).wait_recv()
        v = shard(u).astype(F32)
        mine = jnp.where(net.x == 0, v[:, :half], v[:, half:])
        came = r.xr[u].astype(F32)[:lead]
        first, second = jnp.where(net.x == 0, mine, came), jnp.where(net.x == 0, came, mine)
        w8[u, net.y, net.c, own_rows, own_cols] = jnp.concatenate([first, second], axis=0).astype(BF16)

    def place():
        for k in range(8):
            offer(k)
        pack = r.pack
        pack[...] = jnp.zeros_like(pack)
        for row, one in enumerate((r.bq, None, r.bv, r.bo, r.g1, r.s1, r.b2, r.gg2, r.s2, r.bi1)):
            if one is not None:
                size = one.shape[0]
                pack[row:row + 1, :size] = one[...].astype(F32).reshape(1, size)
        r.small[net.y, net.c, net.z, net.x] = pack[...].astype(BF16)
        w2[net.y, net.c, lax.div(net.z, 2), lax.rem(net.z, 2), pl.ds(pl.multiple_of(net.x * 4 * lead, 16), 4 * lead), :] = (
            r.wouter[...])
        masks()
        turn()
        net.meet()
        for k in range(8):
            swap(k).start()

    l0 = r.lengths[0, 0]
    l1 = l0 + r.lengths[0, 1]
    vec, bi, gsm, cs = r.vec, r.bi, r.gsm, r.cs
    fa, q3 = r.fa, r.q3
    act, gp, act_t = r.act, r.gp, r.act_t

    def loop(body, step=STEP, total=frame_count):
        def one(i, carry):
            body(pl.ds(pl.multiple_of(i * step, step), step))
            return carry

        lax.fori_loop(0, total // step, one, 0)

    def groups(shape, dim, start=0):
        place = lax.broadcasted_iota(jnp.int32, shape, dim) + start
        return (place >= l0).astype(jnp.int32) + (place >= l1).astype(jnp.int32)

    def masks():
        shape = (frame_count, LANES)
        lane = lax.broadcasted_iota(jnp.int32, shape, 1)
        group = groups(shape, 0)
        for e in range(2):
            spare = lane - (1 - e) * (LANES // 2)
            inside = (spare >= 0) & (spare < 3)
            r.mq[e] = jnp.where(inside & (spare != group), -1e30, 0.0).astype(BF16)
            r.mk[e] = jnp.where(inside & (spare == group), 1.0, 0.0).astype(BF16)

    def vectors():
        got = r.small[...].reshape(32 * 16, LANES)
        lane = lax.broadcasted_iota(jnp.int32, (LANES, width), 0)
        col = lax.broadcasted_iota(jnp.int32, (LANES, width), 1)
        tile = jnp.where((lane < lead) & (lane == lax.rem(col, lead)), 1.0, 0.0).astype(BF16)
        wide = mm(got, tile).reshape(32, 16, width)
        owner = lax.broadcasted_iota(jnp.int32, wide.shape, 0)
        place = lax.div(lax.broadcasted_iota(jnp.int32, wide.shape, 2), lead)
        vec[...] = jnp.sum(jnp.where(owner == place, wide, 0.0), axis=0)
        inner = got.astype(F32).reshape(32, 16, LANES)[:, 9, :].astype(BF16)
        for c in range(4):
            lane = lax.broadcasted_iota(jnp.int32, (LANES, width), 0)
            col = lax.broadcasted_iota(jnp.int32, (LANES, width), 1) + c * width
            tile = jnp.where((lane < 4 * lead) & (lane == lax.rem(col, 4 * lead)), 1.0, 0.0).astype(BF16)
            wide = mm(inner, tile)
            owner = lax.broadcasted_iota(jnp.int32, wide.shape, 0)
            place = lax.div(lax.broadcasted_iota(jnp.int32, wide.shape, 1) + c * width, 4 * lead)
            bi[c] = jnp.sum(jnp.where(owner == place, wide, 0.0), axis=0, keepdims=True)

    def square(u):
        return w8[u].reshape(width, width)

    def project(u):
        rows = mm(r.xbuf[...], square(u)) + vec[pl.ds(u, 1), :]
        q3[u] = (rows * jnp.where(u == 0, 0.125, 1.0)).astype(BF16)

    def head_lanes(shape, e):
        return lax.div(lax.broadcasted_iota(jnp.int32, shape, 1), LANES // 2) == e

    ROWS = 256

    def attend(p):
        cols = pl.ds(pl.multiple_of(p * LANES, LANES), LANES)
        sides = []
        for e in range(2):
            mine = head_lanes((frame_count, LANES), e)
            keys = jnp.where(mine, q3[1, :, cols], r.mk[e])
            vals = jnp.where(mine, q3[2, :, cols], jnp.ones((), BF16))
            sides.append((keys, vals))
        for i in range(frame_count // ROWS):
            rows = pl.ds(i * ROWS, ROWS)
            outs = []
            for e in range(2):
                keys, vals = sides[e]
                mine = head_lanes((ROWS, LANES), e)
                query = jnp.where(mine, q3[0, rows, cols], r.mq[e, rows, :])
                scores = mm_nt(query, keys)
                top = jnp.max(scores, axis=1, keepdims=True)
                weights = jnp.exp(scores - top).astype(BF16)
                e12[2 * p + e, rows, :] = weights
                outs.append(mm(weights, vals))
            low = head_lanes((ROWS, LANES), 0)
            over = jnp.where(low, outs[0], outs[1])
            under = pltpu.roll(jnp.where(low, outs[1], outs[0]), LANES // 2, 1)
            inverse = 1.0 / under
            r.linv[rows, cols] = inverse
            r.ctx[rows, cols] = (over * inverse).astype(BF16)

    def norm_one():
        fa[...] = mm(r.ctx[...], square(3))
        r.ctx_t[...] = jnp.transpose(r.ctx[...]).reshape(r.ctx_t.shape)

        def body(rows):
            v = r.xbuf[rows, :].astype(F32) + fa[rows, :] + vec[3:4, :]
            center = v - jnp.mean(v, axis=1, keepdims=True)
            scale = lax.rsqrt(jnp.mean(center * center, axis=1, keepdims=True) + 1e-05)
            normed = center * scale
            r.n1[rows, :] = normed
            r.r1[rows, :] = jnp.broadcast_to(scale, (STEP, LANES))
            r.low[rows, :] = (normed * vec[4:5, :] + vec[5:6, :]).astype(BF16)

        loop(body)
        r.hid_t[...] = jnp.transpose(r.low[...]).reshape(r.hid_t.shape)

    def feed(c):
        fa[...] = mm(r.low[...], square(4 + c))

        def body(rows):
            v = fa[rows, :] + bi[c]
            phi = 0.5 + 0.5 * lax.erf(v * 0.7071067811865476)
            bell = jnp.exp(v * v * -0.5) * 0.3989422804014327
            act[c, rows, :] = (v * phi).astype(BF16)
            gp[c, rows, :] = (phi + v * bell).astype(BF16)

        loop(body, 32)
        act_t[lax.div(c, 2), lax.rem(c, 2)] = jnp.transpose(act[c])

    def block(ref, c):
        return ref[lax.div(c, 2), lax.rem(c, 2)].reshape(width, width)

    def feed_out(k):
        start, size = OUTER[k]
        cols = slice(start, start + size)
        total = None
        for c in range(4):
            one = mm(act[c], w2[c // 2, c % 2, :, :, :, cols].reshape(width, size))
            total = one if total is None else total + one
        fa[:, cols] = total

    def fold(slot, row):
        gsm[pl.ds(row, 1), :] = jnp.sum(cs[slot], axis=0, keepdims=True)

    def norm_two():
        g_in.wait()
        cs[...] = jnp.zeros_like(cs)

        def body(rows):
            hidden = r.n1[rows, :] * vec[4:5, :] + vec[5:6, :]
            v = hidden + fa[rows, :] + vec[6:7, :]
            center = v - jnp.mean(v, axis=1, keepdims=True)
            scale = lax.rsqrt(jnp.mean(center * center, axis=1, keepdims=True) + 1e-05)
            normed = center * scale
            place = lax.broadcasted_iota(jnp.int32, normed.shape, 0) + rows.start
            live = jnp.where(place < l1, 1.0, 0.0)
            r.xbuf[rows, :] = ((normed * vec[7:8, :] + vec[8:9, :]) * live).astype(BF16)
            top = r.gbuf[rows, :].astype(F32) * live
            e = top * vec[7:8, :]
            d = e - jnp.mean(e, axis=1, keepdims=True) - normed * jnp.mean(e * normed, axis=1, keepdims=True)
            d = d * scale
            r.d2[rows, :] = d
            low = d.astype(BF16)
            r.low[rows, :] = low
            cs[0] += eights(top * normed)
            cs[1] += eights(top)
            cs[2] += eights(low.astype(F32))

        loop(body)
        fold(0, 7)
        fold(1, 8)
        fold(2, 6)

    layer_out = pltpu.make_async_copy(r.xbuf, r.layer_out, r.isem.at[0])
    frames_out = pltpu.make_async_copy(r.gbuf, r.frames_grad, r.isem.at[1])

    def back_feed(c):
        fa[...] = mm_nt(r.low[...], block(w2, c))
        cs[0] = jnp.zeros_like(cs[0])

        def body(rows):
            low = (fa[rows, :] * gp[c, rows, :].astype(F32)).astype(BF16)
            gp[c, rows, :] = low
            cs[0] += eights(low.astype(F32))

        loop(body)
        fold(0, 9 + c)

    def grad_square(u, left, right, own):
        core = net.c if own else 1 - net.c
        to = w2.at[u // 2, u % 2] if u < 3 else w8.at[u]
        rows = mm(left[:, core].reshape(2 * pair * NZ, frame_count), right()).reshape(2, pair * NZ, width)
        if own:
            scatter[u].sibling_in().wait_recv()
            rows = rows + to[:, core].astype(F32)
        to[:, core] = rows.astype(BF16)

    def grad_outer(i, own):
        core = net.c if own else 1 - net.c
        start, size = OUTER[i - 8]
        cols = pl.ds(start, size)
        left = act_t[:, core].reshape(2 * width, frame_count)
        rows = mm(left, r.low[:, cols]).reshape((2,) + g2.shape[2:5] + (size,))
        if own:
            scatter[i].sibling_in().wait_recv()
            rows = rows + g2[:, core, :, :, :, cols].astype(F32)
        g2[:, core, :, :, :, cols] = rows.astype(BF16)

    def back_hidden(c):
        got = mm_nt(gp[c], square(4 + c))

        @pl.when(c == 0)
        def _():
            fa[...] = got

        @pl.when(c > 0)
        def _():
            fa[...] += got

    def back_norm_one():
        cs[...] = jnp.zeros_like(cs)

        def body(rows):
            d = r.d2[rows, :] + fa[rows, :]
            normed = r.n1[rows, :]
            e = d * vec[4:5, :]
            cs[0] += eights(d * normed)
            cs[1] += eights(d)
            d = e - jnp.mean(e, axis=1, keepdims=True) - normed * jnp.mean(e * normed, axis=1, keepdims=True)
            d = d * r.r1[rows, 0:1]
            r.d2[rows, :] = d
            low = d.astype(BF16)
            r.low[rows, :] = low
            cs[2] += eights(low.astype(F32))

        loop(body)
        fold(0, 4)
        fold(1, 5)
        fold(2, 3)

    def back_context():
        act[3] = mm_nt(r.low[...], square(3)).astype(BF16)

    def back_attend(p):
        cols = pl.ds(pl.multiple_of(p * LANES, LANES), LANES)
        shape = (frame_count, LANES)
        low = head_lanes(shape, 0)
        scaled = (act[3, :, cols].astype(F32) * r.linv[:, cols]).astype(BF16)
        product = scaled.astype(F32) * r.ctx[:, cols].astype(F32)
        lane = lax.broadcasted_iota(jnp.int32, shape, 1)
        k2, v2, q2 = q3[1, :, cols], q3[2, :, cols], q3[0, :, cols]
        dq, dk, dv = [], [], []
        for e in range(2):
            mine = head_lanes(shape, e)
            spare = lane - (1 - e) * (LANES // 2)
            dot = jnp.sum(jnp.where(mine, product, 0.0), axis=1, keepdims=True)
            high = dot.astype(BF16).astype(F32)
            extra = jnp.where(spare == 0, high, jnp.where(spare == 1, dot - high, 0.0)).astype(BF16)
            left = jnp.where(mine, scaled, extra)
            minus = jnp.where((spare == 0) | (spare == 1), -1.0, 0.0).astype(BF16)
            right = jnp.where(mine, v2, minus)
            for i in range(frame_count // ROWS):
                part = slice(i * ROWS, (i + 1) * ROWS)
                r.ds[e, part, :] = (e12[2 * p + e, part, :].astype(F32) * mm_nt(left[part], right)).astype(BF16)
            dq.append(mm(r.ds[e], k2))
            dk.append(mm_tn(r.ds[e], q2))
            dv.append(mm_tn(e12[2 * p + e], scaled))
        act[0, :, cols] = (jnp.where(low, dq[0], dq[1]) * 0.125).astype(BF16)
        act[1, :, cols] = jnp.where(low, dk[0], dk[1]).astype(BF16)
        act[2, :, cols] = jnp.where(low, dv[0], dv[1]).astype(BF16)

    def bias_sums():
        cs[...] = jnp.zeros_like(cs)

        def body(rows):
            cs[0] += eights(act[0, rows, :].astype(F32))
            cs[1] += eights(act[2, rows, :].astype(F32))

        loop(body)
        fold(0, 0)
        fold(1, 2)
        gsm[1:2, :] = jnp.zeros((1, width), F32)
        gsm[13:16, :] = jnp.zeros((3, width), F32)

    def back_frames(k):
        r.d2[...] += mm_nt(act[k], square(k))

    def frames_ready():
        layer_out.wait()

        def body(rows):
            r.gbuf[rows, :] = r.d2[rows, :].astype(BF16)

        loop(body)
        frames_out.start()

    def small_copy(k, device):
        return pltpu.make_async_remote_copy(
            src_ref=r.sm.at[k], dst_ref=r.sl.at[k], send_sem=r.sms.at[0], recv_sem=r.smr.at[k],
            device_id=device, device_id_type=MESH)

    def small_step(k):
        if k == 0:
            r.sm[0] = gsm[...]
        else:
            r.sm[k] = r.sm[k - 1] + r.sl[k - 1]
        if k < 3:
            small_copy(k, net.across("cyx"[k])).start()

    def small_wait(k):
        small_copy(k, net.across("cyx"[k])).wait_recv()

    def small_line(k):
        return pltpu.make_async_remote_copy(
            src_ref=r.sm.at[3], dst_ref=r.sl.at[2 + k], send_sem=r.sms.at[0], recv_sem=r.smr.at[3],
            device_id=net.dev(z=lax.rem(net.z + k, NZ)), device_id_type=MESH)

    def small_total():
        landed = r.sl.at[pl.ds(3, NZ - 1)]
        pltpu.make_async_remote_copy(
            src_ref=landed, dst_ref=landed, send_sem=r.sms.at[0], recv_sem=r.smr.at[3], device_id=net.across("c"),
            device_id_type=MESH).wait_recv()
        whole = r.sm[3] + r.sl[3] + r.sl[4] + r.sl[5]
        index = (net.y * 2 + net.c) * 2 * NZ + net.z * 2 + net.x
        turned = pltpu.roll(whole, lax.rem(width - index * lead, width), 1)
        row = lax.broadcasted_iota(jnp.int32, (16, width), 0)
        block = lax.div(index, 8)
        inner = jnp.sum(jnp.where(row == 9 + block, whole, 0.0), axis=0, keepdims=True)
        inner = pltpu.roll(jnp.broadcast_to(inner, (8, width)), lax.rem(width - lax.rem(index, 8) * 4 * lead, width), 1)
        r.gsmall[0:8, :] = turned[0:8, :LANES]
        r.gsmall[8:16, :] = jnp.where(row[:8, :LANES] == 0, turned[8:9, :LANES], inner[:, :LANES])

    def swap_back(u):
        return pltpu.make_async_remote_copy(
            src_ref=r.ys.at[u], dst_ref=r.yr.at[u], send_sem=r.yss.at[0], recv_sem=r.yrs.at[0],
            device_id=net.across("x"), device_id_type=MESH)

    def out_of(u):
        if u < 4:
            return (r.gwq, r.gwk, r.gwv, r.gwo)[u], 0
        return r.gwi, (u - 4) * width

    def total_square(u):
        r.f8[...] = scatter[u].total()
        out, start = out_of(u)
        mine, theirs = pl.multiple_of(net.x * lead, 8), pl.multiple_of((1 - net.x) * lead, 8)
        r.ys[u] = jnp.concatenate([r.f8[pl.ds(theirs, lead), :], jnp.zeros((8, half), F32)], axis=0).astype(BF16)
        swap_back(u).start()
        out[:, pl.ds(pl.multiple_of(start + net.x * half, LANES), half)] = r.f8[pl.ds(mine, lead), :]

    def last():
        pltpu.make_async_remote_copy(
            src_ref=r.ys, dst_ref=r.yr, send_sem=r.yss.at[0], recv_sem=r.yrs.at[0], device_id=net.across("x"),
            device_id_type=MESH).wait_recv()
        for u in range(8):
            out, start = out_of(u)
            out[:, pl.ds(pl.multiple_of(start + (1 - net.x) * half, LANES), half)] = r.yr[u].astype(F32)[:lead]

    def total_outer(i):
        r.gwouter[:, pl.ds(*OUTER[i - 8])] = scatter[i].total()

    def unit(i, left=None, right=None):
        steps = SimpleNamespace(**gather[i])
        if i == len(UNITS) - 1:
            return steps
        way, square = scatter[i], i < 8

        def half_of(own):
            if square:
                grad_square(i, left, right, own)
            else:
                grad_outer(i, own)

        def away():
            half_of(False)
            way.sibling_out().start()

        def home():
            half_of(True)
            way.spread()

        steps.away, steps.home = away, home
        steps.t, steps.u, steps.v = way.fold_first, way.fold_second, way.fold_third
        if square:
            steps.p = functools.partial(merge, i)
            steps.x = functools.partial(total_square, i)
        else:
            steps.x = functools.partial(total_outer, i)
        return steps

    def give(k):
        pl.semaphore_signal(r.free.at[k], inc=1, device_id=net.across("c"), device_id_type=MESH)

    def take(k):
        pl.semaphore_wait(r.free.at[k], 1)

    def turn():
        x_in.wait()
        r.xt[...] = jnp.transpose(r.xbuf[...]).reshape(r.xt.shape)

    def gather_end():
        all_sent(r.gout, r.gmate)
        sent(e12.at[0, pl.ds(0, 15 * 16), pl.ds(0, LANES)], r.gout.at[2])
        sent(r.small.at[:, 0], r.gmate.at[2])

    def small(k):
        if k > 0:
            small_wait(k - 1)
        small_step(k)
        if k == 3:
            for one in range(1, NZ):
                small_line(one).start()

    def end():
        all_sent(r.sout, r.smate)
        sent(r.xs, r.xss.at[0])
        sent(r.ys, r.yss.at[0])
        sent(r.sl, r.sms.at[0])
        frames_out.wait()

    def rolled(count, body):
        def one(i, carry):
            body(i)
            return carry

        lax.fori_loop(0, count, one, 0)

    def go(*steps):
        for step in steps:
            step()

    q, k, v = (unit(u, r.xt, lambda u=u: act[u]) for u in range(3))
    o = unit(3, r.ctx_t, lambda: r.low[...])
    i0, i1, i2, i3 = (unit(4 + u, r.hid_t, lambda u=u: gp[u]) for u in range(4))
    w0, w1, w2_, w3 = (unit(8 + u) for u in range(4))
    s = unit(12)
    place()
    go(s.a, w3.a, q.p, q.a, w2_.a, s.b, i1.p, k.p, k.a, i0.p, i0.a, v.p)
    go(w3.b, i2.p, i2.a, s.c, i3.p, i3.a, v.a, o.p, o.a, i1.a, q.b, w0.a)
    go(w3.c, s.d, k.b, s.e, q.c, v.b)
    vectors()
    go(w1.a, k.c, v.c, q.d, o.b, k.d, i1.b, v.d, q.e, i0.b)

    def project_run(i):
        project(i)

        @pl.when(i == 0)
        def _():
            go(v.e, w0.b, o.c, i2.b, k.e)

        @pl.when(i == 1)
        def _():
            go(i3.b, w0.c, i1.c, i0.c)

    rolled(3, project_run)

    def attend_run(i):
        attend(i)

        @pl.when(i == 0)
        def _():
            go(o.d)

        @pl.when(i == 1)
        def _():
            go(w3.d, w0.d, w2_.b)

        @pl.when(i == 2)
        def _():
            go(i2.c, w1.b, i1.d, i0.d)

    rolled(6, attend_run)
    go(o.e, i1.e, w1.c, i3.c)
    norm_one()
    go(w0.e, i0.e)

    def feed_run(i):
        feed(i)

        @pl.when(i == 0)
        def _():
            go(i2.d, w2_.c)

        @pl.when(i == 1)
        def _():
            go(w3.e, i3.d, i2.e)

        @pl.when(i == 2)
        def _():
            go(w1.d, i3.e)

    rolled(4, feed_run)
    go(w2_.d)
    feed_out(3)
    feed_out(0)
    go(w1.e)
    feed_out(1)
    go(w2_.e)
    feed_out(2)
    norm_two()
    go(w3.away, w1.away, w0.away)
    gather_end()
    go(w2_.away, w3.home)

    def back_feed_run(i):
        back_feed(i)

        @pl.when(i == 0)
        def _():
            go(w1.home)

        @pl.when(i == 1)
        def _():
            go(w0.home)

    rolled(4, back_feed_run)
    go(w3.t)
    give(0)

    def back_hidden_run(i):
        back_hidden(i)

        @pl.when(i == 0)
        def _():
            take(0)

    rolled(4, back_hidden_run)
    give(1)
    take(1)
    go(i0.away, w1.t, w0.t, w2_.home, i2.away, i0.home)
    back_norm_one()
    back_context()
    give(2)
    go(i2.home, w0.u, i3.away, w0.v, i1.away)
    take(2)
    go(o.away, w2_.t)

    def back_attend_run(i):
        back_attend(i)

        @pl.when(i == 0)
        def _():
            go(i3.home, i2.t)

        @pl.when(i == 1)
        def _():
            go(i0.t, w2_.u, o.home)

        @pl.when(i == 3)
        def _():
            go(i1.home)

        @pl.when(i == 4)
        def _():
            go(w2_.v)

    rolled(6, back_attend_run)
    go(k.away)
    layer_out.start()
    go(v.away, i2.u, i3.t, i2.v)

    def back_frames_run(i):
        back_frames(i)

        @pl.when(i == 0)
        def _():
            go(k.home, o.t, i1.t, q.away, i3.u, i3.v, w0.x, k.t, v.home, i1.u, i1.v, q.home)
            bias_sums()
            go(v.t, q.t, k.u, k.v, w1.u, q.u, i3.x, o.u)
            small(0)
            go(i1.x, q.v)
            small(1)
            go(i2.x, w3.u, i0.u)

        @pl.when(i == 1)
        def _():
            go(w1.v, o.v, v.u, v.v)
            small(2)
            go(k.x)

    rolled(3, back_frames_run)
    frames_ready()
    small(3)
    go(q.x, w1.x, w3.v, o.x, i0.v, w3.x, v.x, w2_.x, i0.x)
    small_total()
    last()
    end()


def kernel_device(
    frames, lengths, query_weight, query_bias, key_weight, value_weight, value_bias, output_weight, output_bias,
    first_gain, first_shift, inner_weight, inner_bias, outer_weight, outer_bias, second_gain, second_shift, grad_out,
):
    count, width = frames.shape
    lead = query_weight.shape[0]
    pair, half = 2 * lead, width // 2
    vmem, hbm = pl.BlockSpec(memory_space=pltpu.VMEM), pl.BlockSpec(memory_space=pl.ANY)
    smem = pl.BlockSpec(memory_space=pltpu.SMEM)
    args = dict(
        frames=(hbm, frames), grad_out=(hbm, grad_out), lengths=(smem, lengths), wq=(vmem, query_weight),
        wk=(vmem, key_weight), wv=(vmem, value_weight), wo=(vmem, output_weight), wi=(vmem, inner_weight),
        wouter=(vmem, outer_weight), bq=(vmem, query_bias), bv=(vmem, value_bias), bo=(vmem, output_bias),
        g1=(vmem, first_gain), s1=(vmem, first_shift), b2=(vmem, outer_bias), gg2=(vmem, second_gain),
        s2=(vmem, second_shift), bi1=(vmem, inner_bias))
    shape = jax.ShapeDtypeStruct
    outs = dict(
        layer_out=(hbm, shape((count, width), BF16)), frames_grad=(hbm, shape((count, width), BF16)),
        gwq=(vmem, shape((lead, width), F32)), gwk=(vmem, shape((lead, width), F32)),
        gwv=(vmem, shape((lead, width), F32)), gwo=(vmem, shape((lead, width), F32)),
        gwi=(vmem, shape(inner_weight.shape, F32)), gwouter=(vmem, shape(outer_weight.shape, F32)),
        gsmall=(vmem, shape((16, LANES), F32)))
    dma = pltpu.SemaphoreType.DMA
    big = (count, width)
    square = (2, 2, pair * NZ, width)
    turned = (2, 2, pair * NZ, count)
    lead_shape = (2, 2, 2, 2, 8 * lead, width)
    scratch = dict(
        w8=((8,) + square, BF16), w2=(lead_shape, BF16), g2=(lead_shape, BF16), small=((2, 2, NZ, 2, 16, LANES), BF16),
        pack=((16, LANES), F32), xs=((8, lead + 8, half), BF16), xr=((8, lead + 8, half), BF16),
        ys=((8, lead + 8, half), BF16), yr=((8, lead + 8, half), BF16), xbuf=(big, BF16), gbuf=(big, BF16), q3=((3,) + big, BF16),
        e12=((HEADS, count, count), BF16), linv=(big, F32), ctx=(big, BF16), xt=(turned, BF16), ctx_t=(turned, BF16),
        hid_t=(turned, BF16), low=(big, BF16), n1=(big, F32), r1=((count, LANES), F32), act=((4,) + big, BF16),
        gp=((4,) + big, BF16), act_t=((2, 2, width, count), BF16), fa=(big, F32), d2=(big, F32),
        ds=((2, count, count), BF16), mq=((2, count, LANES), BF16), mk=((2, count, LANES), BF16), vec=((16, width), F32),
        bi=((4, 1, width), F32), gsm=((16, width), F32), cs=((3, 8, width), F32), sm=((4, 16, width), F32),
        sl=((6, 16, width), F32), f8=((pair, half), F32))
    for i in range(12):
        for kind, size in zip(LANDING, landing_shapes(i, pair, half, 4 * lead), strict=True):
            scratch[f"{kind}{i}"] = (size, BF16)
    scratch = {k: pltpu.VMEM(*v) for k, v in scratch.items()}
    scratch.update(
        gout=dma((3,)), gmate=dma((3,)), grecv=dma((13, 4)), sout=dma((2,)), smate=dma((2,)), srecv=dma((12, 5)),
        xss=dma((1,)), xrs=dma((8,)), yss=dma((1,)), yrs=dma((1,)), sms=dma((1,)), smr=dma((4,)), isem=dma((2,)), free=pltpu.SemaphoreType.REGULAR((3,)))
    got = pl.pallas_call(
        functools.partial(layer_kernel, (*args, *outs, *scratch)),
        out_shape=[o[1] for o in outs.values()],
        in_specs=[a[0] for a in args.values()],
        out_specs=[o[0] for o in outs.values()],
        scratch_shapes=list(scratch.values()),
        compiler_params=pltpu.CompilerParams(collective_id=0, has_side_effects=True, vmem_limit_bytes=VMEM_BYTES),
    )(*(a[1] for a in args.values()))

    bias, wide = shape((lead,), F32), shape((4 * lead,), F32)
    vectors = {3: bias, 6: bias, 8: bias, 9: bias, 10: bias, 12: wide, 14: bias, 15: bias, 16: bias}
    row_of = {3: 0, 6: 2, 8: 3, 9: 4, 10: 5, 12: 9, 14: 6, 15: 7, 16: 8}
    places = [i for i in range(17) if i not in vectors]

    def publish(*refs):
        came, small, out = refs[:8], refs[8], refs[9:]
        for a, i in zip(came, places, strict=True):
            out[i][...] = a[...]
        for i, row in row_of.items():
            size = vectors[i].shape[0]
            out[i][...] = small[row:row + 1, :size].reshape(size)

    whole = dict(zip(places, (o[1] for o in list(outs.values())[:8]), strict=True))
    return tuple(pl.pallas_call(
        publish,
        out_shape=[vectors[i] if i in vectors else whole[i] for i in range(17)],
        in_specs=[vmem] * 9,
        out_specs=[vmem] * 17,
    )(*got))


VMEM_BYTES = 63 << 20


def solution(mesh):
    split = P(("dp", "fsdp"))
    rows = P(("dp", "fsdp"), None)
    in_specs = (
        rows, rows, rows, split, rows, rows, split, rows, split, split, split, rows, split, rows, split, split, split, rows,
    )
    out_specs = (
        rows, rows, rows, split, rows, rows, split, rows, split, split, split, rows, split, rows, split, split, split,
    )
    fits = mesh.shape["dp"] == 4 and mesh.shape["fsdp"] == 2 * NZ

    def per_device(frames, lengths, query_weight, *rest):
        lead, width = query_weight.shape
        good = fits and lead % 8 == 0 and 4 * lead <= LANES and width == 768
        run = kernel_device if good else general_device
        return run(frames, lengths, query_weight, *rest)

    return jax.shard_map(per_device, mesh=mesh, in_specs=in_specs, out_specs=out_specs, check_vma=False)
```

profile of v0, /device:TPU:24, one launch (start us, length us, event | category | flops | bytes accessed | tf_op | source)
XLA Modules:
  0.0 153.7 jit_solution(17421401779247545168)
XLA Ops:
  0.7 149.8 %shard_map.305 = (bf16[512,768]{1,0:T(8,128)(2,1)}, bf16[512,768]{1,0:T(8,128)(2,1)}, f32[24,768]{1,0:T(8,128)}, f32[24,768]{1,0:T(8,128)}, f32[24,768]{1,0:T(8,...) custom-call(bf16[512,768]{1,0:T(8,128)(2,1)} %refs_0_.1, ...), custom_call_target="tpu_custom_call" | custom-call | tf_op jit(solution)/shard_map/pallas_call | solution.py:1255
  150.4 3.1 %shard_map.306 = (bf16[512,768]{1,0:T(8,128)(2,1)}, bf16[512,768]{1,0:T(8,128)(2,1)}, f32[24,768]{1,0:T(8,128)}, f32[24]{0:T(128)}, f32[24,768]{1,0:T(8,128)}, /...) custom-call(bf16[512,768]{1,0:T(8,128)(2,1)} %get-tuple-element.26.r, ...), custom_call_target="tpu_custom_call" | custom-call | tf_op jit(solution)/shard_map/pallas_call | solution.py:1278
where the time goes:
time: 156 us; the launch traced here: 154 us
  Pallas kernels  153 us (98%)
    pallas_call x1, Pallas kernels, kernel_device(): pl.pallas_call(functools.partial(layer_kernel, (*args, *outs, *scratch)),...  150 us
    pallas_call x1, Pallas kernels, kernel_device(): pl.pallas_call(publish, out_shape=[vectors[i] if i in vectors else whole[...  3.13 us

commit v1 on v0

--- a/solution.py
+++ b/solution.py
@@ -305,17 +305,44 @@
 
 
 class Gather(Way):
-    def __init__(self, net, region, order, sems, bulk):
+    def __init__(self, net, region, order, sems, bulk, line_out):
         super().__init__(net, region, order, sems)
-        self.bulk = bulk
+        self.bulk, self.line_out = bulk, line_out
 
     def lines_start(self, have):
+        n = self.net
         part = self.part(have)
-        for k in range(1, NZ):
-            self.copy(part, part, 0, self.net.dev(z=self.ahead(k))).start()
+        inside = lax.rem(lax.div(n.z + 1, 2), 2)
+        self.copy(part, part, 4 * (1 - inside), n.dev(z=self.ahead(2)), self.line_out).start()
+
+        @pl.when(n.z < NZ - 1)
+        def _():
+            self.copy(part, part, 0, n.dev(z=n.z + 1), self.line_out).start()
+
+        @pl.when(n.z > 0)
+        def _():
+            self.copy(part, part, 0, n.dev(z=n.z - 1), self.line_out).start()
+
+    def lines_pass(self, have):
+        n = self.net
+
+        @pl.when((n.z > 0) & (n.z < NZ - 1))
+        def _():
+            part = self.part(have, z=(NZ - 1) * (2 - n.z))
+            self.wait_for(part, 4)
+            self.copy(part, part, 0, n.dev(z=(NZ - 1) * (n.z - 1)), self.line_out).start()
 
     def lines_wait(self, have):
-        self.wait_for(self.bulk(len(have) * (NZ - 1) + NZ - 1), 0)
+        n = self.net
+        times = 2 if have else 1
+
+        @pl.when((n.z > 0) & (n.z < NZ - 1))
+        def _():
+            self.wait_for(self.bulk(times, 2), 0)
+
+        @pl.when((n.z == 0) | (n.z == NZ - 1))
+        def _():
+            self.wait_for(self.bulk(times, 3), 0)
 
     def over(self, slot, d, have, **at):
         part = self.part(have, **at)
@@ -328,44 +355,38 @@
     def stages(self):
         first, d2, d3 = self.order
 
-        def start_a():
-            self.lines_start("")
-
-        def start_b():
+        def spread():
             self.lines_wait("")
             self.over(1, d2, "z").start()
             self.over(2, d3, "z").start()
 
-        def start_c():
+        def turn():
             self.over(1, d2, "z").wait_recv()
             self.over(2, d3, "z", **self.flip(d2)).start()
 
-        def start_d():
-            self.wait_for(self.part(d2 + "z", **self.flip(d3)), 2)
+        def mate():
+            self.wait_for(self.part((first + d2 if first == "z" else first + "z"), **self.flip(d3)), 2)
             self.sibling().start()
 
-        def start_e():
+        def ready():
             self.sibling().wait_recv()
 
         if first == "z":
-            return dict(a=start_a, b=start_b, c=start_c, d=start_d, e=start_e)
-
-        def begin_a():
+            start, onward = functools.partial(self.lines_start, ""), functools.partial(self.lines_pass, "")
+            return dict(a=start, b=onward, c=spread, d=turn, e=mate, g=ready)
+
+        def begin():
             self.over(1, first, "").start()
 
-        def begin_b():
+        def lines():
             self.over(1, first, "").wait_recv()
             self.lines_start(first)
 
-        def begin_c():
+        def cross():
             self.lines_wait(first)
             self.over(2, d3, first + "z").start()
 
-        def begin_d():
-            self.wait_for(self.part(first + "z", **self.flip(d3)), 2)
-            self.sibling().start()
-
-        return dict(a=begin_a, b=begin_b, c=begin_c, d=begin_d, e=start_e)
+        return dict(a=begin, b=lines, c=functools.partial(self.lines_pass, first), d=cross, e=mate, g=ready)
 
 
 class Scatter(Way):
@@ -488,21 +509,30 @@
 
 def bulk_square(ref):
     pair, half = ref.shape[2] // NZ, ref.shape[3] // 2
-    return lambda k: ref.at[pl.ds(0, k // 3), 0, pl.ds(0, 3 * pair), pl.ds(0, half)]
+    return lambda times, k: ref.at[pl.ds(0, times), 0, pl.ds(0, k * pair), pl.ds(0, half)]
 
 
 def bulk_lead(ref, start, size):
-    rows = 3 * ref.shape[4] // 4
-    return lambda k: ref.at[0, 0, pl.ds(0, k // 3), pl.ds(0, 2), pl.ds(0, rows), pl.ds(start, size)]
+    run = ref.shape[4] // 2
+    return lambda times, k: ref.at[0, 0, pl.ds(0, times), pl.ds(0, 2), pl.ds(0, k * run // 2), pl.ds(start, size)]
 
 
 def bulk_small(ref):
-    return lambda k: ref.at[0, 0, pl.ds(0, k), 0]
+    return lambda times, k: ref.at[0, 0, pl.ds(0, k), 0]
+
+
+def stretch(ref, count, width):
+    deep, tall, _ = ref.shape
+    rows = count // width
+    for a in range(deep, 0, -1):
+        if rows % (16 * a) == 0 and rows // a <= tall:
+            return ref.at[pl.ds(0, a), pl.ds(0, rows // a), pl.ds(0, width)]
+    raise ValueError(count)
 
 
 UNITS = range(13)
-GATHER = ("zxy", "zyx", "zxy", "zyx", "yzx", "zxy", "xzy", "yzx", "zxy", "zxy", "yzx", "zyx", "zxy")
-SCATTER = ("zyx", "zxy", "zxy", "yzx", "yzx", "zxy", "zxy", "zxy", "zxy", "yzx", "zxy", "xzy", "zxy")
+GATHER = ("zyx", "zxy", "zyx", "xzy", "zxy", "yzx", "zxy", "zyx", "xzy", "yzx", "zyx", "zxy", "zxy")
+SCATTER = ("zyx", "zyx", "zxy", "zxy", "xzy", "yzx", "zyx", "zxy", "yzx", "zxy", "yzx", "xzy", "zxy")
 OUTER = ((0, 256), (256, 256), (512, 128), (640, 128))
 
 
@@ -575,7 +605,7 @@
             region, bulk = region_small(r.small), bulk_small(r.small)
         kind = 0 if i < 8 else 1 if cols else 2
         sems = r.gout.at[kind], r.gmate.at[kind], r.grecv.at[i]
-        gather.append(Gather(net, region, GATHER[i], sems, bulk).stages())
+        gather.append(Gather(net, region, GATHER[i], sems, bulk, r.gline.at[kind]).stages())
         if i < 12:
             landing = (getattr(r, f"{name}{i}") for name in LANDING)
             sems = r.sout.at[kind], r.smate.at[kind], r.srecv.at[i]
@@ -586,10 +616,7 @@
             src_ref=ref, dst_ref=ref, send_sem=sem, recv_sem=r.grecv.at[0, 0], device_id=net.across("c"),
             device_id_type=MESH).wait_send()
 
-    def all_sent(out, mate):
-        runs = frame_count - 2 * 16
-        sent(e12.at[pl.ds(0, 12), pl.ds(0, runs), pl.ds(0, half)], out.at[0])
-        sent(r.act.at[pl.ds(0, 3), pl.ds(0, runs), :], out.at[1])
+    def mates_sent(mate):
         sent(w8.at[:, :, 0], mate.at[0])
         sent(w2.at[:, 0], mate.at[1])
 
@@ -922,9 +949,9 @@
 
     def small_step(k):
         if k == 0:
-            r.sm[0] = gsm[...]
+            r.sm[0] = gsm[...].astype(BF16)
         else:
-            r.sm[k] = r.sm[k - 1] + r.sl[k - 1]
+            r.sm[k] = (r.sm[k - 1].astype(F32) + r.sl[k - 1].astype(F32)).astype(BF16)
         if k < 3:
             small_copy(k, net.across("cyx"[k])).start()
 
@@ -941,7 +968,7 @@
         pltpu.make_async_remote_copy(
             src_ref=landed, dst_ref=landed, send_sem=r.sms.at[0], recv_sem=r.smr.at[3], device_id=net.across("c"),
             device_id_type=MESH).wait_recv()
-        whole = r.sm[3] + r.sl[3] + r.sl[4] + r.sl[5]
+        whole = sum((r.sl[k].astype(F32) for k in range(3, 6)), r.sm[3].astype(F32))
         index = (net.y * 2 + net.c) * 2 * NZ + net.z * 2 + net.x
         turned = pltpu.roll(whole, lax.rem(width - index * lead, width), 1)
         row = lax.broadcasted_iota(jnp.int32, (16, width), 0)
@@ -1020,8 +1047,18 @@
         r.xt[...] = jnp.transpose(r.xbuf[...]).reshape(r.xt.shape)
 
     def gather_end():
-        all_sent(r.gout, r.gmate)
-        sent(e12.at[0, pl.ds(0, 15 * 16), pl.ds(0, LANES)], r.gout.at[2])
+        kinds = ((range(8), pair * half, half), (range(8, 12), lead * 4 * LANES, 2 * LANES), (range(12, 13), 16 * LANES, LANES))
+        for kind, (units, count, run) in enumerate(kinds):
+            flat = lines = 0
+            for i in units:
+                size = count * (OUTER[i - 8][1] // LANES if kind == 1 else 1)
+                flat += size * (12 if GATHER[i][0] == "z" else 9)
+                lines += size * (2 if GATHER[i][0] == "z" else 4)
+            sent(stretch(e12, flat, run), r.gout.at[kind])
+            inside = (net.z > 0) & (net.z < NZ - 1)
+            for way, times in ((inside, 2), (jnp.logical_not(inside), 1)):
+                pl.when(way)(functools.partial(sent, stretch(e12, lines * times, run), r.gline.at[kind]))
+        mates_sent(r.gmate)
         sent(r.small.at[:, 0], r.gmate.at[2])
 
     def small(k):
@@ -1033,7 +1070,9 @@
                 small_line(one).start()
 
     def end():
-        all_sent(r.sout, r.smate)
+        sent(stretch(e12, 8 * 15 * pair * half, half), r.sout.at[0])
+        sent(stretch(e12, 15 * 4 * lead * width, 2 * LANES), r.sout.at[1])
+        mates_sent(r.smate)
         sent(r.xs, r.xss.at[0])
         sent(r.ys, r.yss.at[0])
         sent(r.sl, r.sms.at[0])
@@ -1056,153 +1095,151 @@
     w0, w1, w2_, w3 = (unit(8 + u) for u in range(4))
     s = unit(12)
     place()
-    go(s.a, w3.a, q.p, q.a, w2_.a, s.b, i1.p, k.p, k.a, i0.p, i0.a, v.p)
-    go(w3.b, i2.p, i2.a, s.c, i3.p, i3.a, v.a, o.p, o.a, i1.a, q.b, w0.a)
-    go(w3.c, s.d, k.b, s.e, q.c, v.b)
+    go(w3.a, w1.a, w3.b, s.a, q.p, q.a, w3.c, s.b, q.b, v.p, i1.p, i1.a)
+    go(k.p, i0.p, k.a, q.c, v.a, w0.a, k.b, w3.d, s.c, k.c, w2_.a, i3.p)
+    go(i0.a, q.d, o.p, o.a, i2.p, w3.e, s.d, v.b, i3.a, k.d, i2.a, s.e)
+    go(i0.b, v.c, i0.c, o.b, w3.g, q.e, q.g, i2.b, s.g, k.e, i3.b, v.d)
     vectors()
-    go(w1.a, k.c, v.c, q.d, o.b, k.d, i1.b, v.d, q.e, i0.b)
+    go(i1.b, i3.c)
 
     def project_run(i):
         project(i)
 
         @pl.when(i == 0)
         def _():
-            go(v.e, w0.b, o.c, i2.b, k.e)
+            go(k.g, o.c)
 
         @pl.when(i == 1)
         def _():
-            go(i3.b, w0.c, i1.c, i0.c)
+            go(i0.d, i2.c, v.e, w1.b, o.d, i1.c, v.g, i3.d)
 
     rolled(3, project_run)
+    go(w2_.b)
 
     def attend_run(i):
         attend(i)
 
-        @pl.when(i == 0)
-        def _():
-            go(o.d)
-
         @pl.when(i == 1)
         def _():
-            go(w3.d, w0.d, w2_.b)
-
-        @pl.when(i == 2)
-        def _():
-            go(i2.c, w1.b, i1.d, i0.d)
+            go(w0.b, i1.d)
+
+        @pl.when(i == 4)
+        def _():
+            go(w1.c, i2.d, i0.e, i3.e, w1.d, w2_.c, w0.c, o.e)
 
     rolled(6, attend_run)
-    go(o.e, i1.e, w1.c, i3.c)
+    go(w0.d, i0.g, i1.e, o.g)
     norm_one()
-    go(w0.e, i0.e)
+    go(i2.e)
 
     def feed_run(i):
         feed(i)
 
         @pl.when(i == 0)
         def _():
-            go(i2.d, w2_.c)
+            go(w2_.d, i1.g, i2.g)
 
         @pl.when(i == 1)
         def _():
-            go(w3.e, i3.d, i2.e)
+            go(w1.e)
 
         @pl.when(i == 2)
         def _():
-            go(w1.d, i3.e)
+            go(i3.g, w0.e)
 
     rolled(4, feed_run)
-    go(w2_.d)
+    go(w2_.e, w1.g)
+    feed_out(1)
     feed_out(3)
+    go(w0.g)
     feed_out(0)
-    go(w1.e)
-    feed_out(1)
-    go(w2_.e)
+    go(w2_.g)
     feed_out(2)
     norm_two()
-    go(w3.away, w1.away, w0.away)
+    go(w2_.away)
     gather_end()
-    go(w2_.away, w3.home)
+    go(w3.away, w0.away, w1.away, w2_.home)
 
     def back_feed_run(i):
         back_feed(i)
 
-        @pl.when(i == 0)
-        def _():
-            go(w1.home)
-
         @pl.when(i == 1)
         def _():
-            go(w0.home)
+            go(w3.home, w0.home)
+
+        @pl.when(i == 2)
+        def _():
+            go(w2_.t, w1.home)
 
     rolled(4, back_feed_run)
-    go(w3.t)
-    give(0)
 
     def back_hidden_run(i):
         back_hidden(i)
 
         @pl.when(i == 0)
         def _():
-            take(0)
+            go(w3.t)
 
     rolled(4, back_hidden_run)
     give(1)
+    layer_out.start()
     take(1)
-    go(i0.away, w1.t, w0.t, w2_.home, i2.away, i0.home)
+    go(i0.away, w1.t)
+    give(0)
+    go(i1.away, w0.t)
     back_norm_one()
+    go(i0.home, i2.away, i1.home, i3.away)
     back_context()
-    give(2)
-    go(i2.home, w0.u, i3.away, w0.v, i1.away)
-    take(2)
-    go(o.away, w2_.t)
+    go(w1.u, w1.v)
 
     def back_attend_run(i):
         back_attend(i)
 
         @pl.when(i == 0)
         def _():
-            go(i3.home, i2.t)
+            give(2)
+            take(2)
+            go(i3.home, i2.home, o.away)
 
         @pl.when(i == 1)
         def _():
-            go(i0.t, w2_.u, o.home)
+            take(0)
+
+        @pl.when(i == 2)
+        def _():
+            go(i1.t, o.home)
 
         @pl.when(i == 3)
         def _():
-            go(i1.home)
-
-        @pl.when(i == 4)
-        def _():
-            go(w2_.v)
+            go(i0.t, i3.t, i2.t)
 
     rolled(6, back_attend_run)
-    go(k.away)
-    layer_out.start()
-    go(v.away, i2.u, i3.t, i2.v)
+    go(w1.x, q.away, o.t)
 
     def back_frames_run(i):
         back_frames(i)
 
         @pl.when(i == 0)
         def _():
-            go(k.home, o.t, i1.t, q.away, i3.u, i3.v, w0.x, k.t, v.home, i1.u, i1.v, q.home)
+            go(i2.u, v.away, q.home)
             bias_sums()
-            go(v.t, q.t, k.u, k.v, w1.u, q.u, i3.x, o.u)
+            go(v.home, k.away, i2.v, o.u, k.home, i3.u, i3.v, q.t, q.u, o.v, k.t, i0.u)
+            go(q.v)
             small(0)
-            go(i1.x, q.v)
+            go(v.t, w2_.u, i1.u, k.u, i2.x, i0.v, v.u, k.v)
             small(1)
-            go(i2.x, w3.u, i0.u)
+            go(w3.u, i3.x)
 
         @pl.when(i == 1)
         def _():
-            go(w1.v, o.v, v.u, v.v)
+            go(i1.v)
             small(2)
-            go(k.x)
+            go(v.v, w0.u, q.x, w3.v, i1.x)
+            small(3)
+            go(w2_.v, o.x, i0.x, w0.v, k.x, w2_.x, v.x, w0.x, w3.x)
 
     rolled(3, back_frames_run)
     frames_ready()
-    small(3)
-    go(q.x, w1.x, w3.v, o.x, i0.v, w3.x, v.x, w2_.x, i0.x)
     small_total()
     last()
     end()
@@ -1243,14 +1280,14 @@
         hid_t=(turned, BF16), low=(big, BF16), n1=(big, F32), r1=((count, LANES), F32), act=((4,) + big, BF16),
         gp=((4,) + big, BF16), act_t=((2, 2, width, count), BF16), fa=(big, F32), d2=(big, F32),
         ds=((2, count, count), BF16), mq=((2, count, LANES), BF16), mk=((2, count, LANES), BF16), vec=((16, width), F32),
-        bi=((4, 1, width), F32), gsm=((16, width), F32), cs=((3, 8, width), F32), sm=((4, 16, width), F32),
-        sl=((6, 16, width), F32), f8=((pair, half), F32))
+        bi=((4, 1, width), F32), gsm=((16, width), F32), cs=((3, 8, width), F32), sm=((4, 16, width), BF16),
+        sl=((6, 16, width), BF16), f8=((pair, half), F32))
     for i in range(12):
         for kind, size in zip(LANDING, landing_shapes(i, pair, half, 4 * lead), strict=True):
             scratch[f"{kind}{i}"] = (size, BF16)
     scratch = {k: pltpu.VMEM(*v) for k, v in scratch.items()}
     scratch.update(
-        gout=dma((3,)), gmate=dma((3,)), grecv=dma((13, 4)), sout=dma((2,)), smate=dma((2,)), srecv=dma((12, 5)),
+        gout=dma((3,)), gline=dma((3,)), gmate=dma((3,)), grecv=dma((13, 5)), sout=dma((2,)), smate=dma((2,)), srecv=dma((12, 5)),
         xss=dma((1,)), xrs=dma((8,)), yss=dma((1,)), yrs=dma((1,)), sms=dma((1,)), smr=dma((4,)), isem=dma((2,)), free=pltpu.SemaphoreType.REGULAR((3,)))
     got = pl.pallas_call(
         functools.partial(layer_kernel, (*args, *outs, *scratch)),

time: 156 us -> 152 us (0.974)
  Pallas kernels: 153 us -> 149 us
    pallas_call x1, Pallas kernels: 150 us -> 146 us  [kernel_device(): pl.pallas_call(functools.partial(layer_kernel, (*args, *outs, *scratch)),...]
where the time goes in v1:
time: 152 us; the launch traced here: 150 us
  Pallas kernels  149 us (98%)
    pallas_call x1, Pallas kernels, kernel_device(): pl.pallas_call(functools.partial(layer_kernel, (*args, *outs, *scratch)),...  146 us
    pallas_call x1, Pallas kernels, kernel_device(): pl.pallas_call(publish, out_shape=[vectors[i] if i in vectors else whole[...  3.13 us

profile of v1, /device:TPU:24, one launch (start us, length us, event | category | flops | bytes accessed | tf_op | source)
XLA Modules:
  0.0 149.6 jit_solution(15344442569839268628)
XLA Ops:
  0.7 145.6 %shard_map.305 = (bf16[512,768]{1,0:T(8,128)(2,1)}, bf16[512,768]{1,0:T(8,128)(2,1)}, f32[24,768]{1,0:T(8,128)}, f32[24,768]{1,0:T(8,128)}, f32[24,768]{1,0:T(8,...) custom-call(bf16[512,768]{1,0:T(8,128)(2,1)} %refs_0_.1, ...), custom_call_target="tpu_custom_call" | custom-call | tf_op jit(solution)/shard_map/pallas_call | solution.py:1292
  146.3 3.1 %shard_map.306 = (bf16[512,768]{1,0:T(8,128)(2,1)}, bf16[512,768]{1,0:T(8,128)(2,1)}, f32[24,768]{1,0:T(8,128)}, f32[24]{0:T(128)}, f32[24,768]{1,0:T(8,128)}, /...) custom-call(bf16[512,768]{1,0:T(8,128)(2,1)} %get-tuple-element.26.r, ...), custom_call_target="tpu_custom_call" | custom-call | tf_op jit(solution)/shard_map/pallas_call | solution.py:1315

commit v2 on v1

--- a/solution.py
+++ b/solution.py
@@ -571,7 +571,7 @@
     return jnp.sum(block.reshape(block.shape[0] // 8, 8, block.shape[1]), axis=0)
 
 
-STEP = 64
+STEP = 128
 F32, BF16 = jnp.float32, jnp.bfloat16
 
 
@@ -772,7 +772,7 @@
             act[c, rows, :] = (v * phi).astype(BF16)
             gp[c, rows, :] = (phi + v * bell).astype(BF16)
 
-        loop(body, 32)
+        loop(body, 64)
         act_t[lax.div(c, 2), lax.rem(c, 2)] = jnp.transpose(act[c])
 
     def block(ref, c):

time: 152 us -> 151 us (level)
  no operation moved by 1% of the time
where the time goes in v2:
time: 151 us; the launch traced here: 149 us
  Pallas kernels  148 us (98%)
    pallas_call x1, Pallas kernels, kernel_device(): pl.pallas_call(functools.partial(layer_kernel, (*args, *outs, *scratch)),...  145 us
    pallas_call x1, Pallas kernels, kernel_device(): pl.pallas_call(publish, out_shape=[vectors[i] if i in vectors else whole[...  3.13 us

profile of v2, /device:TPU:24, one launch (start us, length us, event | category | flops | bytes accessed | tf_op | source)
XLA Modules:
  0.0 148.5 jit_solution(1608291334724876668)
XLA Ops:
  0.7 144.5 %shard_map.305 = (bf16[512,768]{1,0:T(8,128)(2,1)}, bf16[512,768]{1,0:T(8,128)(2,1)}, f32[24,768]{1,0:T(8,128)}, f32[24,768]{1,0:T(8,128)}, f32[24,768]{1,0:T(8,...) custom-call(bf16[512,768]{1,0:T(8,128)(2,1)} %refs_0_.1, ...), custom_call_target="tpu_custom_call" | custom-call | tf_op jit(solution)/shard_map/pallas_call | solution.py:1292
  145.2 3.1 %shard_map.306 = (bf16[512,768]{1,0:T(8,128)(2,1)}, bf16[512,768]{1,0:T(8,128)(2,1)}, f32[24,768]{1,0:T(8,128)}, f32[24]{0:T(128)}, f32[24,768]{1,0:T(8,128)}, /...) custom-call(bf16[512,768]{1,0:T(8,128)(2,1)} %get-tuple-element.26.r, ...), custom_call_target="tpu_custom_call" | custom-call | tf_op jit(solution)/shard_map/pallas_call | solution.py:1315
